TPU v7x, 512 devices: a whole 4x4x16 slice. The times are simulated.
512 devices in a mesh: gx: 32 (over z, core), gy: 16 (over y, x).
Axes of the slice: x: 4, y: 4, z: 16, core: 2. Of those that a mesh axis runs over, the one named last changes fastest.
Arguments:
- rhs_leaf: float32 [32, 16, 8, 512], P('gx', 'gy'), may hold values from -6 to 6
- leaf_inv: float32 [32, 16, 4, 128, 128], P('gx', 'gy'), may hold values from -0.5 to 0.5
- leaf_sub: float32 [32, 16, 3, 128, 128], P('gx', 'gy'), may hold values from -0.375 to 0.375
- sep_rhs: float32 [32, 16, 8, 96], P('gx', 'gy'), may hold values from -6 to 6
- interface: int32 [32, 16, 4, 128], P('gx', 'gy'), may hold values from 0 to 8191, as said below
- coupling: float32 [32, 16, 4, 128, 512], P('gx', 'gy'), may hold values from -0.125 to 0.125
- factor_one: float32 [32, 16, 16, 8192], P('gx', 'gy'), may hold values from -0.0625 to 0.0625
- factor_two: float32 [32, 16, 16, 4096], P('gx', 'gy'), may hold values from -0.09375 to 0.09375
- factor_three: float32 [32, 16, 32, 4096], P('gx', 'gy'), may hold values from -0.09375 to 0.09375
- factor_four: float32 [32, 16, 32, 2048], P('gx', 'gy'), may hold values from -0.125 to 0.125
- link_two: float32 [32, 16, 16, 128], P('gx', 'gy'), may hold values from -0.375 to 0.375
- link_three: float32 [32, 16, 32, 128], P('gx', 'gy'), may hold values from -0.25 to 0.25
- link_four: float32 [32, 16, 32, 128], P('gx', 'gy'), may hold values from -0.25 to 0.25
Outputs:
- leaf_solution: float32 [32, 16, 8, 512], P('gx', 'gy')
- sep_solution: float32 [32, 16, 8, 96], P('gx', 'gy')
Inputs may be any that keep to these rules, and one draw needn't show every extreme that they name: interface[a, c, k-1, n] is a position of a level-k separator, below S_k, and S_k - 1 is reached at every level; positions may repeat within a leaf.
All inputs are finite; a program needn't handle non-finite values.
Results may differ from a plain program's by a relative error of at most 0.00014.
Values sent between devices are 32-bit elements; how exact they have to be, the bound alone decides.
A program may use at most 64 MiB of HBM per device.

v0:
```python
import jax
import jax.numpy as jnp
from jax import lax
from jax.sharding import PartitionSpec as P

PRECISE = lax.Precision.HIGHEST


def from_partner(value, axis, distance):
    return lax.ppermute(value, axis, [(i, i ^ 1 << distance) for i in range(lax.axis_size(axis))])


def taken_lists(gy_bits, gx_bits):
    first = list(range(gy_bits + gx_bits))
    second = [bit_number for bit_number in first if bit_number != gy_bits + gx_bits - 1]
    third = [bit_number for bit_number in second if bit_number != gy_bits - 1]
    fourth = [bit_number for bit_number in third if bit_number != gy_bits + gx_bits - 2]
    return [first, second, third, fourth]


def rank_in_group(device_index, taken):
    group_rank = jnp.zeros((), jnp.int32)
    for bit_number in sorted(taken, reverse=True):
        group_rank = group_rank * 2 + (device_index >> bit_number & 1)
    return group_rank


def group_total(values, section, taken):
    if section == 0:
        return lax.psum(values, ("gx", "gy"))
    for bit_number in sorted(taken, reverse=True):
        values = values + from_partner(values, ("gx", "gy"), bit_number)
    return values


def leaf_forward(right_side, inverse_blocks, lower_blocks):
    block_size = inverse_blocks.shape[1]
    results = []
    earlier = None
    for counter in range(inverse_blocks.shape[0]):
        current = right_side[:, counter * block_size : (counter + 1) * block_size]
        if counter > 0:
            current = current - jnp.dot(earlier, lower_blocks[counter - 1], precision=PRECISE)
        earlier = jnp.dot(current, inverse_blocks[counter], precision=PRECISE)
        results.append(earlier)
    return jnp.concatenate(results, axis=1)


def leaf_backward(leaf_work, inverse_blocks, lower_blocks):
    block_size = inverse_blocks.shape[1]
    block_count = inverse_blocks.shape[0]
    contract_last = (((1,), (1,)), ((), ()))
    results = [None] * block_count
    later = None
    for counter in reversed(range(block_count)):
        current = leaf_work[:, counter * block_size : (counter + 1) * block_size]
        if counter < block_count - 1:
            current = current - lax.dot_general(
                later, lower_blocks[counter], contract_last, precision=PRECISE
            )
        later = lax.dot_general(current, inverse_blocks[counter], contract_last, precision=PRECISE)
        results[counter] = later
    return jnp.concatenate(results, axis=1)


def local(
    rhs_leaf,
    leaf_inv,
    leaf_sub,
    sep_rhs,
    interface,
    coupling,
    factor_one,
    factor_two,
    factor_three,
    factor_four,
    link_two,
    link_three,
    link_four,
):
    contract_last = (((1,), (1,)), ((), ()))
    gy_bits = lax.axis_size("gy").bit_length() - 1
    gx_bits = lax.axis_size("gx").bit_length() - 1
    sections = taken_lists(gy_bits, gx_bits)
    device_index = lax.axis_index(("gx", "gy"))
    factors = (factor_one[0, 0], factor_two[0, 0], factor_three[0, 0], factor_four[0, 0])
    link_mats = (link_two[0, 0], link_three[0, 0], link_four[0, 0])
    places = interface[0, 0]
    couplings = coupling[0, 0]
    own_rhs = sep_rhs[0, 0]
    inverse_blocks = leaf_inv[0, 0]
    lower_blocks = leaf_sub[0, 0]
    forward = leaf_forward(rhs_leaf[0, 0], inverse_blocks, lower_blocks)
    rhs_count = forward.shape[0]
    offsets = [0]
    for section in range(3):
        offsets.append(offsets[-1] + factors[section].shape[0])
    ranks = [rank_in_group(device_index, taken) for taken in sections]
    own_z = [None] * 4
    for section in (3, 2, 1, 0):
        own_rows, sep_width = factors[section].shape
        partials_in = lax.dot_general(forward, couplings[section], contract_last, precision=PRECISE)
        if section < 3:
            partials_in = partials_in + jnp.dot(
                own_z[section + 1], link_mats[section], precision=PRECISE
            )
        contribution = jnp.zeros((rhs_count, sep_width), jnp.float32)
        own_part = own_rhs[:, offsets[section] : offsets[section] + own_rows]
        contribution = lax.dynamic_update_slice(
            contribution, own_part, (jnp.zeros((), jnp.int32), ranks[section] * own_rows)
        )
        contribution = contribution.at[:, places[section]].add(-partials_in)
        summed = group_total(contribution, section, sections[section])
        own_z[section] = lax.dot_general(summed, factors[section], contract_last, precision=PRECISE)
    full_sep = [None] * 4
    own_x = []
    for section in range(4):
        own_rows = factors[section].shape[0]
        update = own_z[section]
        if section > 0:
            picked = full_sep[section - 1][:, places[section - 1]]
            update = update - lax.dot_general(
                picked, link_mats[section - 1], contract_last, precision=PRECISE
            )
        partial_value = jnp.dot(update, factors[section], precision=PRECISE)
        full_sep[section] = group_total(partial_value, section, sections[section])
        own_x.append(
            lax.dynamic_slice_in_dim(full_sep[section], ranks[section] * own_rows, own_rows, 1)
        )
    leaf_work = forward
    for section in range(4):
        picked = full_sep[section][:, places[section]]
        leaf_work = leaf_work - jnp.dot(picked, couplings[section], precision=PRECISE)
    leaf_solution = leaf_backward(leaf_work, inverse_blocks, lower_blocks)
    sep_solution = jnp.concatenate(own_x, axis=1)
    return (leaf_solution[None, None], sep_solution[None, None])


def solution(mesh):
    in_specs = (
        P("gx", "gy", None, None),
        P("gx", "gy", None, None, None),
        P("gx", "gy", None, None, None),
        P("gx", "gy", None, None),
        P("gx", "gy", None, None),
        P("gx", "gy", None, None, None),
        P("gx", "gy", None, None),
        P("gx", "gy", None, None),
        P("gx", "gy", None, None),
        P("gx", "gy", None, None),
        P("gx", "gy", None, None),
        P("gx", "gy", None, None),
        P("gx", "gy", None, None),
    )
    out_specs = (P("gx", "gy", None, None), P("gx", "gy", None, None))
    return jax.shard_map(local, mesh=mesh, in_specs=in_specs, out_specs=out_specs, check_vma=False)
```

profile of v0, /device:TPU:1, one launch (start us, length us, event | category | flops | bytes accessed | tf_op | source)
XLA Modules:
  0.0 1343.3 jit_solution(9264529725911563697)
XLA Ops:
  19.3 3.4 scatter_fusion
  24.2 5.7 collective-permute-start
  31.6 3.5 collective-permute-start.1
  37.1 9.2 collective-permute-start.2
  54.1 4.6 collective-permute-done.4
  66.9 5.2 collective-permute-start.6
  72.1 13.9 %collective-permute-done.6 = f32[8,4096]{1,0:T(8,128)S(1)} collective-permute-done((f32[8,4096]{1,0:T(8,128)S(1)}, f32[8,4096]{1,0:T(8,128)S(1)}, u32[]{:S(2)}, u32[]{:S(2)}) %collective-permute-start.6) | collective-permute-done | bytes 131104 | tf_op jit(solution)/shard_map/ppermute | solution.py:10
  87.9 6.0 collective-permute-done.7
  95.8 3.8 collective-permute-done.8
  99.6 4.1 collective-permute-start.9
  104.7 3.7 collective-permute-start.10
  108.5 3.5 collective-permute-done.10
  112.0 4.5 collective-permute-start.11
  129.5 3.5 collective-permute-start.13
  133.0 16.0 %collective-permute-done.13 = f32[8,4096]{1,0:T(8,128)S(1)} collective-permute-done((f32[8,4096]{1,0:T(8,128)S(1)}, f32[8,4096]{1,0:T(8,128)S(1)}, u32[]{:S(2)}, u32[]{:S(2)}) %collective-permute-start.13) | collective-permute-done | bytes 131104 | tf_op jit(solution)/shard_map/ppermute | solution.py:10
  151.0 5.4 collective-permute-done.14
  158.3 3.8 collective-permute-done.15
  162.1 4.4 collective-permute-start.16
  167.5 4.8 collective-permute-start.17
  172.4 3.3 collective-permute-done.17
  175.7 3.2 collective-permute-start.18
  181.4 4.4 collective-permute-start.19
  195.0 5.3 scatter_fusion.3
  200.6 490.6 %all-reduce.3.cloned.1.call-done = f32[8,8192]{0,1:T(8,128)} async-done(((f32[8,8192]{0,1:T(8,128)}), f32[8,8192]{0,1:T(8,128)}) %all-reduce.3.cloned.1.call-update) | async-done | bytes 262160 | tf_op jit(solution)/shard_map/psum | solution.py:30
  691.2 8.9 fusion.11
  701.2 455.7 %all-reduce.5.cloned.1.call-done = f32[8,8192]{1,0:T(8,128)} async-done(((f32[8,8192]{1,0:T(8,128)}), f32[8,8192]{1,0:T(8,128)}) %all-reduce.5.cloned.1.call-update) | async-done | bytes 262160 | tf_op jit(solution)/shard_map/psum | solution.py:30
  1157.0 3.5 copy.84
  1163.8 3.9 collective-permute-start.21
  1167.7 14.8 %collective-permute-done.21 = f32[8,4096]{1,0:T(8,128)S(1)} collective-permute-done((f32[8,4096]{1,0:T(8,128)S(1)}, f32[8,4096]{1,0:T(8,128)S(1)}, u32[]{:S(2)}, u32[]{:S(2)}) %collective-permute-start.21) | collective-permute-done | bytes 131104 | tf_op jit(solution)/shard_map/ppermute | solution.py:10
  1184.5 5.4 collective-permute-done.22
  1191.9 3.8 collective-permute-done.23
  1195.7 4.4 collective-permute-start.24
  1201.1 4.7 collective-permute-start.25
  1205.8 3.4 collective-permute-done.25
  1209.2 3.6 collective-permute-start.26
  1215.2 4.5 collective-permute-start.27
  1233.0 4.0 collective-permute-start.29
  1236.9 14.5 %collective-permute-done.29 = f32[8,4096]{1,0:T(8,128)S(1)} collective-permute-done((f32[8,4096]{1,0:T(8,128)S(1)}, f32[8,4096]{1,0:T(8,128)S(1)}, u32[]{:S(2)}, u32[]{:S(2)}) %collective-permute-start.29) | collective-permute-done | bytes 131104 | tf_op jit(solution)/shard_map/ppermute | solution.py:10
  1253.4 6.4 collective-permute-done.30
  1261.9 3.8 collective-permute-done.31
  1265.7 4.3 collective-permute-start.32
  1271.0 3.5 collective-permute-start.33
  1274.5 3.4 collective-permute-done.33
  1277.9 4.4 collective-permute-start.34
  1297.6 4.7 collective-permute-done.36
  1307.3 7.2 collective-permute-start.38
  1315.4 3.3 collective-permute-start.39
  1320.4 4.5 collective-permute-start.40
  (204 shorter events, 132.0 us)
Async XLA Ops:
  7.2 684.0 %copy-start = (f32[1,1,16,8192]{3,2,1,0:T(8,128)S(1)}, f32[1,1,16,8192]{3,2,1,0:T(8,128)}, u32[]{:S(2)}) copy-start(f32[1,1,16,8192]{3,2,1,0:T(8,128)} %param.19) | copy-start | bytes 1572868
  7.2 684.0 %all-reduce.3.cloned.1.call-start = ((), (), s32[]{:S(2)}) async-start(), calls=%async_computation | async-start | bytes 8388608 | tf_op jit(solution)/shard_map/psum | solution.py:30
  18.0 108.9 %copy-start.22 = (s32[128]{0:T(128)}, s32[128]{0:T(128)S(1)}, u32[]{:S(2)}) copy-start(s32[128]{0:T(128)S(1)} %get-tuple-element.7) | copy-start | bytes 1540
  24.2 7.4 collective-permute-start
  31.6 5.5 collective-permute-start.1
  37.1 10.1 collective-permute-start.2
  47.2 5.0 collective-permute-start.3
  52.2 6.5 collective-permute-start.4
  58.7 5.0 collective-permute-start.5
  66.9 19.1 %collective-permute-start.6 = (f32[8,4096]{1,0:T(8,128)S(1)}, f32[8,4096]{1,0:T(8,128)S(1)}, u32[]{:S(2)}, u32[]{:S(2)}) collective-permute-start(f32[8,4096]{1,0:T(8,128)S(1)} %copy.79), channel_id=1, source_target_pairs={{0,128},{1,129},{2,130},{3,131},{4,132},{5,133},{6,134},{7,135},{8... | collective-permute-start | bytes 393224 | tf_op jit(solution)/shard_map/ppermute | solution.py:10
  86.0 7.9 collective-permute-start.7
  93.9 5.7 collective-permute-start.8
  99.6 5.1 collective-permute-start.9
  104.7 7.2 collective-permute-start.10
  112.0 7.5 collective-permute-start.11
  119.6 5.7 collective-permute-start.12
  128.9 65.4 %copy-start.5 = (f32[1,1,16,4096]{3,2,1,0:T(8,128)S(1)}, f32[1,1,16,4096]{3,2,1,0:T(8,128)}, u32[]{:S(2)}) copy-start(f32[1,1,16,4096]{3,2,1,0:T(8,128)} %param.20) | copy-start | bytes 786436
  129.5 65.5 %copy-start.24 = (s32[128]{0:T(128)S(1)}, s32[128]{0:T(128)}, u32[]{:S(2)}) copy-start(s32[128]{0:T(128)} %get-tuple-element.6) | copy-start | bytes 1540
  129.5 19.5 %collective-permute-start.13 = (f32[8,4096]{1,0:T(8,128)S(1)}, f32[8,4096]{1,0:T(8,128)S(1)}, u32[]{:S(2)}, u32[]{:S(2)}) collective-permute-start(f32[8,4096]{1,0:T(8,128)S(1)} %copy.82), channel_id=1, source_target_pairs={{0,128},{1,129},{2,130},{3,131},{4,132},{5,133},{6,134},{7,135},{8... | collective-permute-start | bytes 393224 | tf_op jit(solution)/shard_map/ppermute | solution.py:10
  149.0 7.4 collective-permute-start.14
  156.4 5.7 collective-permute-start.15
  162.1 5.4 collective-permute-start.16
  167.5 8.1 collective-permute-start.17
  175.7 5.7 collective-permute-start.18
  181.4 7.2 collective-permute-start.19
  188.6 5.7 collective-permute-start.20
  200.3 956.7 %all-reduce.5.cloned.1.call-start = ((), (), s32[]{:S(2)}) async-start(), calls=%async_computation.1 | async-start | bytes 524288 | tf_op jit(solution)/shard_map/psum | solution.py:30
  1163.8 18.7 %collective-permute-start.21 = (f32[8,4096]{1,0:T(8,128)S(1)}, f32[8,4096]{1,0:T(8,128)S(1)}, u32[]{:S(2)}, u32[]{:S(2)}) collective-permute-start(f32[8,4096]{1,0:T(8,128)S(1)} %fusion.17), channel_id=1, source_target_pairs={{0,128},{1,129},{2,130},{3,131},{4,132},{5,133},{6,134},{7,135},{8... | collective-permute-start | bytes 393224 | tf_op jit(solution)/shard_map/ppermute | solution.py:10
  1182.5 7.4 collective-permute-start.22
  1189.9 5.7 collective-permute-start.23
  1195.7 5.4 collective-permute-start.24
  1201.1 8.1 collective-permute-start.25
  1209.2 5.9 collective-permute-start.26
  1215.2 7.2 collective-permute-start.27
  1222.4 5.7 collective-permute-start.28
  1233.0 18.5 %collective-permute-start.29 = (f32[8,4096]{1,0:T(8,128)S(1)}, f32[8,4096]{1,0:T(8,128)S(1)}, u32[]{:S(2)}, u32[]{:S(2)}) collective-permute-start(f32[8,4096]{1,0:T(8,128)S(1)} %fusion.13), channel_id=1, source_target_pairs={{0,128},{1,129},{2,130},{3,131},{4,132},{5,133},{6,134},{7,135},{8... | collective-permute-start | bytes 393224 | tf_op jit(solution)/shard_map/ppermute | solution.py:10
  1251.4 8.4 collective-permute-start.30
  1259.8 5.8 collective-permute-start.31
  1265.7 5.2 collective-permute-start.32
  1271.0 6.9 collective-permute-start.33
  1277.9 7.2 collective-permute-start.34
  1285.2 5.7 collective-permute-start.35
  1295.6 6.6 collective-permute-start.36
  1302.2 5.0 collective-permute-start.37
  1307.3 8.1 collective-permute-start.38
  1315.4 5.0 collective-permute-start.39
  1320.4 6.5 collective-permute-start.40
  1326.9 5.0 collective-permute-start.41
  (21 other events, 733.1 us)
Sparse Core Ops, SparseCore 0:
  200.5 490.6 all-reduce.2
  701.4 455.5 all-reduce.4
where the time goes:
time: 1350 us; the launch traced here: 1340 us
  waiting for transfers between devices  1110 us (82%)
  starting transfers between devices  148 us (11%)
  matrix products  26.8 us (2%)
  local copies, waits for them, and re-layouts  25.8 us (2%)
  other arithmetic  16 us (1%)
  between operations  15 us (1%)
    psum x2, waiting for transfers between devices, group_total(): return lax.psum(values, ('gx', 'gy'))  946 us
    ppermute x42, waiting for transfers between devices, from_partner(): lax.ppermute(value, axis, [(i, i ^ 1 << distance) for i in range(lax.axis...  166 us
    ppermute x42, starting transfers between devices, from_partner(): lax.ppermute(value, axis, [(i, i ^ 1 << distance) for i in range(lax.axis...  147 us
  transfers between devices with their start and end apart: 44, of which 44 were waited for; matrix products, arithmetic and copies ran while one was open for 1% of the time, Pallas kernels for 0%

commit v1 on v0

v1 whole, which is shorter than its diff:
```python
import functools

import jax
import jax.numpy as jnp
from jax import lax
from jax.experimental import pallas as pl
from jax.experimental.pallas import tpu as pltpu
from jax.sharding import PartitionSpec as P

MESH = pl.DeviceIdType.MESH
F32 = jnp.float32
BF16 = jnp.bfloat16
HIGHEST = lax.Precision.HIGHEST
NN = (((1,), (0,)), ((), ()))
NT = (((1,), (1,)), ((), ()))
TILE = 128
NX, NY, NC, NZ = 4, 4, 2, 16


def dense(a, b, dims=NN):
    return lax.dot_general(a, b, dims, precision=HIGHEST, preferred_element_type=F32)


def fast(a, b, dims=NN):
    return lax.dot_general(a, b, dims, preferred_element_type=F32)


def halves(v):
    high = v.astype(BF16).astype(F32)
    return high, v - high


class Level:
    def __init__(self, own, width, off, ny, nz, scatter, exchange):
        self.own = own
        self.width = width
        self.tiles = width // TILE
        self.off = off
        self.size = {"x": NX, "y": ny, "c": NC, "z": nz}
        self.scatter = scatter
        self.exchange = exchange
        self.n_scatter = self.count(scatter)
        self.n_exchange = self.count(exchange)
        self.share = self.tiles // self.n_scatter

    def count(self, axes):
        n = 1
        for axis in axes:
            n *= self.size[axis]
        return n

    def steps(self, axes):
        out = [{}]
        for axis in axes:
            out = [dict(o, **{axis: d}) for d in range(self.size[axis]) for o in out]
        return out[1:]


LEVELS = (
    Level(16, 8192, 0, 4, 16, "xyc", "z"),
    Level(16, 4096, 16, 4, 8, "xyc", "z"),
    Level(32, 4096, 32, 2, 8, "xyc", "z"),
    Level(32, 2048, 64, 2, 4, "xc", "yz"),
)


def kernel(
    rhs_h, inv_h, sub_h, sep_h, pos_h, cpl_h, f1_h, f2_h, f3_h, f4_h, l2_h, l3_h, l4_h,
    leaf_out, sep_out,
    rhs, inv, sub, sep, pos, cpl, f1, f2, f3, f4, l2, l3, l4,
    fwd, base, place_t, place, owned, zval, vmat, cv, work,
    *rest,
):
    bufs = rest[:8]
    in_sem, send_sem, recv_sem = rest[8][0], rest[8][1], rest[8][2]
    factors = (f1, f2, f3, f4)
    links = (l2, l3, l4)

    a, c = lax.axis_index("gx"), lax.axis_index("gy")
    index = a * 16 + c
    here = {"x": lax.rem(c, 4), "y": lax.div(c, 4), "c": lax.rem(a, 2), "z": lax.div(a, 2)}

    def moved(level, step):
        there = dict(here)
        for axis, d in step.items():
            if d:
                n = level.size[axis]
                v = here[axis]
                full = {"x": NX, "y": NY, "c": NC, "z": NZ}[axis]
                if n == full:
                    there[axis] = lax.rem(v + d, n)
                else:
                    inside = lax.rem(v, n)
                    there[axis] = v - inside + lax.rem(inside + d, n)
        return there

    def device(there):
        return (there["z"] * 2 + there["c"], there["y"] * 4 + there["x"])

    def share_of(level, there):
        r = 0
        for axis in level.scatter:
            r = r * level.size[axis] + lax.rem(there[axis], level.size[axis])
        return r

    low = lax.rem(index, 256)
    ranks = (
        index,
        low,
        lax.div(low, 16) * 8 + lax.rem(index, 8),
        lax.div(lax.rem(index, 128), 16) * 8 + lax.rem(index, 8),
    )

    pairs = (
        (rhs_h, rhs), (inv_h, inv), (sub_h, sub), (pos_h, pos), (cpl_h, cpl), (sep_h, sep),
        (f4_h, f4), (l4_h, l4), (f3_h, f3), (l3_h, l3), (f2_h, f2), (l2_h, l2), (f1_h, f1),
    )
    copies = [pltpu.make_async_copy(s, d, in_sem.at[n]) for n, (s, d) in enumerate(pairs)]
    for copy in copies:
        copy.start()

    barrier = pltpu.get_barrier_semaphore()
    greet = {}
    for level in LEVELS:
        for axes in (level.exchange, level.scatter):
            for step in level.steps(axes):
                key = (axes, tuple(sorted(step.items())))
                if axes == "z" and level.size["z"] < NZ:
                    continue
                if axes == "xyc" and level.size["y"] < NY:
                    continue
                if axes == "xc":
                    continue
                if axes == "yz" and (step["y"] == 0):
                    continue
                if axes == "yz" and (step["z"] == 0):
                    continue
                greet[key] = (level, step)
    for level, step in greet.values():
        pl.semaphore_signal(barrier, inc=1, device_id=device(moved(level, step)), device_id_type=MESH)

    for n in range(3):
        copies[n].wait()
    earlier = None
    for j in range(4):
        current = rhs[:, j * TILE : (j + 1) * TILE]
        if j:
            current = current - dense(earlier, sub[j - 1])
        earlier = dense(current, inv[j])
        fwd[:, j * TILE : (j + 1) * TILE] = earlier
    for n in range(3, 6):
        copies[n].wait()

    def prepare(k):
        level = LEVELS[k]
        row = pos[k : k + 1, :]
        lane = lax.rem(row, TILE)
        hot = jnp.broadcast_to(lane, (TILE, TILE)) == lax.broadcasted_iota(jnp.int32, (TILE, TILE), 0)
        hot = jnp.where(hot, 1.0, 0.0)
        turned = jnp.transpose(hot).astype(BF16)
        hot = hot.astype(BF16)
        place_t[k] = jnp.concatenate([hot, hot], axis=0)
        place[k] = jnp.concatenate([turned, turned], axis=0)
        base[k] = dense(fwd[...], cpl[k], NT)
        owned[k] = dense(sep[...], select(k))

    def select(k):
        level = LEVELS[k]
        start = lax.rem(ranks[k] * level.own, TILE)
        q = lax.broadcasted_iota(jnp.int32, (96, TILE), 0) - level.off
        lane = lax.broadcasted_iota(jnp.int32, (96, TILE), 1)
        hit = (q + start == lane) & (q >= 0) & (q < level.own)
        return jnp.where(hit, 1.0, 0.0)

    def tile_of(k):
        row = jnp.broadcast_to(lax.div(pos[k : k + 1, :], TILE), (8, TILE))
        tiles = LEVELS[k].tiles
        return jnp.broadcast_to(row[None], (tiles, 8, TILE)) == lax.broadcasted_iota(
            jnp.int32, (tiles, 8, TILE), 0
        )

    def own_tile(k):
        return lax.div(ranks[k] * LEVELS[k].own, TILE)

    def scatter(k, term, out):
        tiles = LEVELS[k].tiles
        hit = tile_of(k)
        high, lo = halves(-term)
        parts = [
            jnp.where(hit, jnp.broadcast_to(v[None], (tiles, 8, TILE)), 0.0).reshape(tiles * 8, TILE).astype(BF16)
            for v in (high, lo)
        ]
        out[...] = fast(jnp.concatenate(parts, axis=1), place[k]).reshape(tiles, 8, TILE)
        at = pl.ds(own_tile(k), 1)
        out[at] = out[at] + owned[k][None]

    def gather(k, full):
        tiles = LEVELS[k].tiles
        high, lo = halves(full[...].reshape(tiles * 8, TILE))
        got = fast(jnp.concatenate([high.astype(BF16), lo.astype(BF16)], axis=1), place_t[k])
        return jnp.sum(jnp.where(tile_of(k), got.reshape(tiles, 8, TILE), 0.0), axis=0)

    def remote(src, dst, slot, phase, target):
        return pltpu.make_async_remote_copy(
            src_ref=src, dst_ref=dst, send_sem=send_sem.at[slot, phase], recv_sem=recv_sem.at[slot, phase],
            device_id=target, device_id_type=MESH,
        )

    me = (a, c)
    leftover = []

    def total(k, slot, beside=(None, None, None)):
        level = LEVELS[k]
        w = level.share
        part, got, mine, seen, full = bufs[2 * k + slot]
        s = 2 * k + slot
        own = share_of(level, here)
        peers = [moved(level, step) for step in level.steps(level.scatter)]
        for n, there in enumerate(peers):
            remote(part.at[pl.ds(share_of(level, there) * w, w)], got.at[n], s, 0, device(there)).start()
        if beside[0]:
            beside[0]()
        remote(got, got, s, 0, me).wait_recv()
        value = part[pl.ds(own * w, w)] + jnp.sum(got[...], axis=0)
        mine[...] = value
        for n, step in enumerate(level.steps(level.exchange)):
            remote(mine, seen.at[n], s, 1, device(moved(level, step))).start()
        if beside[1]:
            beside[1]()
        remote(seen, seen, s, 1, me).wait_recv()
        at = pl.ds(own * w, w)
        full[at] = mine[...] + jnp.sum(seen[...], axis=0)
        for there in peers:
            remote(full.at[at], full.at[at], s, 2, device(there)).start()
        if beside[2]:
            beside[2]()
        rest_of = full.at[pl.ds(0, level.tiles - w)]
        remote(rest_of, rest_of, s, 2, me).wait_recv()

        def finish():
            remote(rest_of, rest_of, s, 0, me).wait_send()
            remote(seen, seen, s, 1, me).wait_send()
            remote(got, got, s, 2, me).wait_send()

        leftover.append(finish)

    def times_rows(k, full):
        factor = factors[k]
        m = LEVELS[k].own

        def body(j, sums):
            tile = full[j]
            rows = factor[:, pl.ds(pl.multiple_of(j * TILE, TILE), TILE)]
            return tuple(sums[q] + tile * rows[q : q + 1, :] for q in range(m))

        sums = lax.fori_loop(0, LEVELS[k].tiles, body, tuple(jnp.zeros((8, TILE), F32) for _ in range(m)), unroll=4)
        return [jnp.sum(v, axis=1, keepdims=True) for v in sums]

    def spread(k, values, out):
        factor = factors[k]
        m = LEVELS[k].own
        wide = [jnp.broadcast_to(v, (8, TILE)) for v in values]

        def body(j, _):
            rows = factor[:, pl.ds(pl.multiple_of(j * TILE, TILE), TILE)]
            acc = wide[0] * rows[0:1, :]
            for q in range(1, m):
                acc = acc + wide[q] * rows[q : q + 1, :]
            out[j] = acc
            return 0

        lax.fori_loop(0, LEVELS[k].tiles, body, 0, unroll=4)

    def inverse_blocks():
        vmat[...] = jnp.zeros_like(vmat)
        for j in range(4):
            vmat[j * TILE : (j + 1) * TILE, j * TILE : (j + 1) * TILE] = inv[j]
        for j in (2, 1, 0):
            step = -dense(inv[j], sub[j])
            vmat[j * TILE : (j + 1) * TILE, (j + 1) * TILE :] = dense(
                step, vmat[(j + 1) * TILE : (j + 2) * TILE, (j + 1) * TILE :]
            )

    def coupled():
        cv[...] = dense(cpl[3], vmat[...], NT)

    prepare(3)
    scatter(3, base[3], bufs[6][0])
    pl.semaphore_wait(barrier, len(greet))

    def others():
        for k in (2, 1, 0):
            prepare(k)

    besides = {3: (others, inverse_blocks, coupled)}
    first_copy = {3: 6, 2: 8, 1: 10, 0: 12}
    for k in (3, 2, 1, 0):
        total(k, 0, besides.get(k, (None, None, None)))
        m = LEVELS[k].own
        copies[first_copy[k]].wait()
        if k:
            copies[first_copy[k] + 1].wait()
        values = times_rows(k, bufs[2 * k][4])
        if k:
            term = base[k - 1]
            for q in range(m):
                term = term + values[q] * links[k - 1][q : q + 1, :]
            scatter(k - 1, term, bufs[2 * (k - 1)][0])
            for q in range(m):
                zval[LEVELS[k].off + q] = jnp.broadcast_to(values[q], (8, TILE))

    picked = None
    for k in range(4):
        m = LEVELS[k].own
        if k:
            values = [
                zval[LEVELS[k].off + q]
                - jnp.sum(picked * links[k - 1][q : q + 1, :], axis=1, keepdims=True)
                for q in range(m)
            ]
        spread(k, values, bufs[2 * k + 1][0])

        def after(k=k, picked=picked):
            if k == 0:
                work[...] = fwd[...]
                sep_out[...] = jnp.zeros_like(sep_out)
                return
            work[...] = work[...] - dense(picked, cpl[k - 1])
            sep_out[...] = sep_out[...] + dense(bufs[2 * k - 1][4][pl.ds(own_tile(k - 1), 1)][0], select(k - 1), NT)
            if k == 3:
                work[...] = dense(work[...], vmat[...], NT)

        total(k, 1, (after, None, None))
        picked = gather(k, bufs[2 * k + 1][4])
    leaf_out[...] = work[...] - dense(picked, cv[...])
    sep_out[...] = sep_out[...] + dense(bufs[7][4][pl.ds(own_tile(3), 1)][0], select(3), NT)
    for finish in leftover:
        finish()


def local(*args):
    ins = [x[0, 0] for x in args]
    order = ins
    vmem = [pltpu.VMEM(x.shape, x.dtype) for x in order]
    bufs = []
    for level in LEVELS:
        w = level.share
        shapes = (
            (level.tiles, 8, TILE),
            (level.n_scatter - 1, w, 8, TILE),
            (w, 8, TILE),
            (level.n_exchange - 1, w, 8, TILE),
            (level.tiles, 8, TILE),
        )
        for _ in range(2):
            bufs.append(tuple(pltpu.VMEM(s, F32) for s in shapes))
    scratch = vmem + [
        pltpu.VMEM((8, 512), F32),
        pltpu.VMEM((4, 8, TILE), F32),
        pltpu.VMEM((4, 2 * TILE, TILE), BF16),
        pltpu.VMEM((4, 2 * TILE, TILE), BF16),
        pltpu.VMEM((4, 8, TILE), F32),
        pltpu.VMEM((96, 8, TILE), F32),
        pltpu.VMEM((512, 512), F32),
        pltpu.VMEM((TILE, 512), F32),
        pltpu.VMEM((8, 512), F32),
    ]
    sems = (
        pltpu.SemaphoreType.DMA((13,)),
        pltpu.SemaphoreType.DMA((8, 3)),
        pltpu.SemaphoreType.DMA((8, 3)),
    )
    leaf, sep = pl.pallas_call(
        kernel,
        out_shape=(jax.ShapeDtypeStruct((8, 512), F32), jax.ShapeDtypeStruct((8, 96), F32)),
        in_specs=[pl.BlockSpec(memory_space=pl.ANY)] * len(ins),
        out_specs=(pl.BlockSpec(memory_space=pltpu.VMEM),) * 2,
        scratch_shapes=scratch + bufs + [sems],
        compiler_params=pltpu.CompilerParams(
            collective_id=0, has_side_effects=True, vmem_limit_bytes=40 * 1024 * 1024
        ),
        name="nested_solve",
    )(*ins)
    return leaf[None, None], sep[None, None]


def solution(mesh):
    four = P("gx", "gy", None, None)
    five = P("gx", "gy", None, None, None)
    in_specs = (four, five, five, four, four, five) + (four,) * 7
    return jax.shard_map(local, mesh=mesh, in_specs=in_specs, out_specs=(four, four), check_vma=False)
```

time: 1350 us -> 168 us (0.12)
  waiting for transfers between devices: 1110 us -> 0 us
  Pallas kernels: 0 us -> 155 us
  starting transfers between devices: 148 us -> 0 us
  matrix products: 26.8 us -> 0 us
  other arithmetic: 16 us -> 0 us
  between operations: 15 us -> 0.67 us
  local copies, waits for them, and re-layouts: 25.8 us -> 11.8 us
    psum x2 -> x0, waiting for transfers between devices: 946 us -> none  [group_total(): return lax.psum(values, ('gx', 'gy'))]
    ppermute x42 -> x0, waiting for transfers between devices: 166 us -> none  [from_partner(): lax.ppermute(value, axis, [(i, i ^ 1 << distance) for i in range(lax.axis...]
    pallas_call x0 -> x1, Pallas kernels: none -> 155 us  [local(): pl.pallas_call(kernel, out_shape=(jax.ShapeDtypeStruct((8, 512), F32), ja...]
    ppermute x42 -> x0, starting transfers between devices: 147 us -> none  [from_partner(): lax.ppermute(value, axis, [(i, i ^ 1 << distance) for i in range(lax.axis...]
    dot_general x36 -> x0, matrix products: 26.8 us -> none  [the longest x4 10 us: local(): lax.dot_general(summed, factors[section], contract_last, precision=PRECISE)]
  transfers between devices with their start and end apart: 44 -> 0, of which waited for: 44 -> 0; matrix products, arithmetic and copies ran while one was open for 1% -> 0% of each run, Pallas kernels for 0% -> 0%
where the time goes in v1:
time: 168 us
  Pallas kernels  155 us (92%)
  local copies, waits for them, and re-layouts  11.8 us (7%)
    pallas_call x1, Pallas kernels, local(): pl.pallas_call(kernel, out_shape=(jax.ShapeDtypeStruct((8, 512), F32), ja...  155 us
    unnamed x28, local copies, waits for them, and re-layouts  11.8 us

profile of v1, /device:TPU:1, one launch (start us, length us, event | category | flops | bytes accessed | tf_op | source)
XLA Modules:
  0.0 167.8 jit_solution(1561984540578557950)
XLA Ops:
  0.6 0.0 copy-start.7
  0.6 0.0 copy-start.10
  0.7 0.7 copy-done.7
  1.4 0.0 copy-done.10
  1.4 0.0 copy-start
  1.4 1.2 copy-done
  2.6 0.0 copy-start.1
  2.6 1.0 copy-done.1
  3.6 0.0 copy-start.2
  3.6 1.0 copy-done.2
  4.7 0.0 copy-start.3
  4.7 0.9 copy-done.3
  5.6 0.0 copy-start.4
  5.6 0.9 copy-done.4
  6.6 0.0 copy-start.5
  6.6 0.9 copy-done.5
  7.5 0.0 copy-start.6
  7.5 0.9 copy-done.6
  8.4 0.0 copy-start.8
  8.4 0.7 copy-done.8
  9.2 0.0 copy-start.9
  9.2 0.7 copy-done.9
  9.9 0.0 copy-start.11
  9.9 0.7 copy-done.11
  10.6 0.0 copy-start.12
  10.6 0.7 copy-done.12
  11.3 155.4 %nested_solve.1 = (f32[8,512]{1,0:T(8,128)S(1)}, f32[8,96]{1,0:T(8,128)S(1)}) custom-call(f32[8,512]{1,0:T(8,128)S(1)} %bitcast.22, f32[4,128,128]{2,1,0:T(8,128)S(1)} %bitcast.18, f32[3,128,128]{2,1,0:T(8,128)S(1)} %bitcast.21, f32[8,96]{1,0:T(8,128)S(1)} %bitcast.27, s32[4,128]{1,0:T(4,128)S(1)} %bitcast.29, f32[4,128,512]{2,1,0:T(8,128)S(1)} %bitcast.15, ...), custom_call_target="tpu_custom_call" | custom-call | tf_op jit(solution)/shard_map/nested_solve/pallas_call | solution.py:373
  166.6 0.6 copy.17
  167.3 0.6 copy.18
Async XLA Ops:
  0.6 0.7 copy-start.7
  0.6 0.7 copy-start.10
  1.4 1.2 copy-start
  2.6 1.0 copy-start.1
  3.6 1.0 copy-start.2
  4.7 0.9 copy-start.3
  5.6 0.9 copy-start.4
  6.6 0.9 copy-start.5
  7.5 0.9 copy-start.6
  8.4 0.7 copy-start.8
  9.2 0.7 copy-start.9
  9.9 0.7 copy-start.11
  10.6 0.7 copy-start.12

commit v2 on v1

--- a/solution.py
+++ b/solution.py
@@ -31,37 +31,38 @@
 
 
 class Level:
-    def __init__(self, own, width, off, ny, nz, scatter, exchange):
+    def __init__(self, own, width, off, scatter, exchange):
         self.own = own
         self.width = width
         self.tiles = width // TILE
         self.off = off
-        self.size = {"x": NX, "y": ny, "c": NC, "z": nz}
         self.scatter = scatter
         self.exchange = exchange
-        self.n_scatter = self.count(scatter)
-        self.n_exchange = self.count(exchange)
-        self.share = self.tiles // self.n_scatter
-
-    def count(self, axes):
-        n = 1
-        for axis in axes:
-            n *= self.size[axis]
-        return n
-
-    def steps(self, axes):
-        out = [{}]
-        for axis in axes:
-            out = [dict(o, **{axis: d}) for d in range(self.size[axis]) for o in out]
-        return out[1:]
+        self.share = self.tiles >> len(scatter)
 
 
 LEVELS = (
-    Level(16, 8192, 0, 4, 16, "xyc", "z"),
-    Level(16, 4096, 16, 4, 8, "xyc", "z"),
-    Level(32, 4096, 32, 2, 8, "xyc", "z"),
-    Level(32, 2048, 64, 2, 4, "xc", "yz"),
+    Level(16, 8192, 0, (0, 1, 2, 3, 4, 5), (6, 7, 8)),
+    Level(16, 4096, 16, (0, 1, 2, 3, 4), (5, 6, 7)),
+    Level(32, 4096, 32, (0, 1, 2, 4), (5, 6, 7)),
+    Level(32, 2048, 64, (0, 1, 4), (2, 5, 6)),
 )
+SPARSE = (0, 1, 2, 5, 6)
+CORE = (4,)
+
+
+def hops(mask):
+    def ring(n, m):
+        return max(min(abs(v - (v ^ m)), n - abs(v - (v ^ m))) for v in range(n))
+
+    return ring(4, mask & 3) + ring(4, mask >> 2 & 3) + ring(16, mask >> 5) + 0.1 * (mask >> 4 & 1)
+
+
+def masks_of(bits):
+    out = [0]
+    for b in bits:
+        out = out + [m | 1 << b for m in out]
+    return sorted(out[1:], key=lambda m: (-hops(m), m))
 
 
 def kernel(
@@ -78,29 +79,25 @@
 
     a, c = lax.axis_index("gx"), lax.axis_index("gy")
     index = a * 16 + c
-    here = {"x": lax.rem(c, 4), "y": lax.div(c, 4), "c": lax.rem(a, 2), "z": lax.div(a, 2)}
-
-    def moved(level, step):
-        there = dict(here)
-        for axis, d in step.items():
-            if d:
-                n = level.size[axis]
-                v = here[axis]
-                full = {"x": NX, "y": NY, "c": NC, "z": NZ}[axis]
-                if n == full:
-                    there[axis] = lax.rem(v + d, n)
+    bit = [lax.rem(lax.div(index, 1 << j), 2) for j in range(9)]
+    flip = [1 - 2 * v for v in bit]
+
+    def device(mask):
+        x, y = a, c
+        for j in range(9):
+            if mask >> j & 1:
+                if j < 4:
+                    y = y + flip[j] * (1 << j)
                 else:
-                    inside = lax.rem(v, n)
-                    there[axis] = v - inside + lax.rem(inside + d, n)
-        return there
-
-    def device(there):
-        return (there["z"] * 2 + there["c"], there["y"] * 4 + there["x"])
-
-    def share_of(level, there):
+                    x = x + flip[j] * (1 << (j - 4))
+        return (x, y)
+
+    def ordinal(bits, mask=0):
         r = 0
-        for axis in level.scatter:
-            r = r * level.size[axis] + lax.rem(there[axis], level.size[axis])
+        for n, j in enumerate(bits):
+            r = r + bit[j] * (1 << n)
+            if mask >> j & 1:
+                r = r + flip[j] * (1 << n)
         return r
 
     low = lax.rem(index, 256)
@@ -112,7 +109,8 @@
     )
 
     pairs = (
-        (rhs_h, rhs), (inv_h, inv), (sub_h, sub), (pos_h, pos), (cpl_h, cpl), (sep_h, sep),
+        (sep_h, sep), (pos_h, pos), (rhs_h, rhs), (inv_h, inv), (sub_h, sub),
+        (cpl_h.at[3], cpl.at[3]), (cpl_h.at[pl.ds(0, 3)], cpl.at[pl.ds(0, 3)]),
         (f4_h, f4), (l4_h, l4), (f3_h, f3), (l3_h, l3), (f2_h, f2), (l2_h, l2), (f1_h, f1),
     )
     copies = [pltpu.make_async_copy(s, d, in_sem.at[n]) for n, (s, d) in enumerate(pairs)]
@@ -120,36 +118,11 @@
         copy.start()
 
     barrier = pltpu.get_barrier_semaphore()
-    greet = {}
+    greet = set(masks_of(SPARSE)) | set(masks_of(CORE))
     for level in LEVELS:
-        for axes in (level.exchange, level.scatter):
-            for step in level.steps(axes):
-                key = (axes, tuple(sorted(step.items())))
-                if axes == "z" and level.size["z"] < NZ:
-                    continue
-                if axes == "xyc" and level.size["y"] < NY:
-                    continue
-                if axes == "xc":
-                    continue
-                if axes == "yz" and (step["y"] == 0):
-                    continue
-                if axes == "yz" and (step["z"] == 0):
-                    continue
-                greet[key] = (level, step)
-    for level, step in greet.values():
-        pl.semaphore_signal(barrier, inc=1, device_id=device(moved(level, step)), device_id_type=MESH)
-
-    for n in range(3):
-        copies[n].wait()
-    earlier = None
-    for j in range(4):
-        current = rhs[:, j * TILE : (j + 1) * TILE]
-        if j:
-            current = current - dense(earlier, sub[j - 1])
-        earlier = dense(current, inv[j])
-        fwd[:, j * TILE : (j + 1) * TILE] = earlier
-    for n in range(3, 6):
-        copies[n].wait()
+        greet |= set(masks_of(level.scatter)) | set(masks_of(level.exchange))
+    for mask in sorted(greet, key=lambda m: (-hops(m), m)):
+        pl.semaphore_signal(barrier, inc=1, device_id=device(mask), device_id_type=MESH)
 
     def prepare(k):
         level = LEVELS[k]
@@ -161,8 +134,10 @@
         hot = hot.astype(BF16)
         place_t[k] = jnp.concatenate([hot, hot], axis=0)
         place[k] = jnp.concatenate([turned, turned], axis=0)
-        base[k] = dense(fwd[...], cpl[k], NT)
-        owned[k] = dense(sep[...], select(k))
+        if k < 3:
+            base[k] = dense(fwd[...], cpl[k], NT)
+        if k < 3:
+            owned[k] = dense(sep[...], select(k))
 
     def select(k):
         level = LEVELS[k]
@@ -209,38 +184,99 @@
     me = (a, c)
     leftover = []
 
-    def total(k, slot, beside=(None, None, None)):
+    def total(k, slot, beside=None):
         level = LEVELS[k]
         w = level.share
         part, got, mine, seen, full = bufs[2 * k + slot]
         s = 2 * k + slot
-        own = share_of(level, here)
-        peers = [moved(level, step) for step in level.steps(level.scatter)]
-        for n, there in enumerate(peers):
-            remote(part.at[pl.ds(share_of(level, there) * w, w)], got.at[n], s, 0, device(there)).start()
-        if beside[0]:
-            beside[0]()
+        at = pl.ds(ordinal(level.scatter) * w, w)
+        peers = masks_of(level.scatter)
+        for n, mask in enumerate(peers):
+            theirs = pl.ds(ordinal(level.scatter, mask) * w, w)
+            remote(part.at[theirs], got.at[n], s, 0, device(mask)).start()
+        if beside:
+            beside()
         remote(got, got, s, 0, me).wait_recv()
-        value = part[pl.ds(own * w, w)] + jnp.sum(got[...], axis=0)
-        mine[...] = value
-        for n, step in enumerate(level.steps(level.exchange)):
-            remote(mine, seen.at[n], s, 1, device(moved(level, step))).start()
-        if beside[1]:
-            beside[1]()
+        mine[...] = part[at] + jnp.sum(got[...], axis=0)
+        for n, mask in enumerate(masks_of(level.exchange)):
+            remote(mine, seen.at[n], s, 1, device(mask)).start()
         remote(seen, seen, s, 1, me).wait_recv()
-        at = pl.ds(own * w, w)
         full[at] = mine[...] + jnp.sum(seen[...], axis=0)
-        for there in peers:
-            remote(full.at[at], full.at[at], s, 2, device(there)).start()
-        if beside[2]:
-            beside[2]()
-        rest_of = full.at[pl.ds(0, level.tiles - w)]
-        remote(rest_of, rest_of, s, 2, me).wait_recv()
+        for mask in peers:
+            remote(full.at[at], full.at[at], s, 2, device(mask)).start()
+        others = full.at[pl.ds(0, level.tiles - w)]
+        remote(others, others, s, 2, me).wait_recv()
 
         def finish():
-            remote(rest_of, rest_of, s, 0, me).wait_send()
+            remote(others, others, s, 0, me).wait_send()
             remote(seen, seen, s, 1, me).wait_send()
             remote(got, got, s, 2, me).wait_send()
+
+        leftover.append(finish)
+
+    crowd = masks_of(SPARSE)
+    n_crowd = len(crowd)
+    early, terms, hots, owns, half, other, top = bufs[6]
+
+    def introduce():
+        owned_row = dense(sep[...], select(3))
+        early[n_crowd, 0:8, :] = owned_row
+        early[n_crowd, 8:9, :] = pos[3:4, :].astype(F32)
+        for n, mask in enumerate(crowd):
+            remote(early.at[n_crowd], early.at[n], 6, 0, device(mask)).start()
+
+    def send_terms():
+        terms[n_crowd] = -dense(fwd[...], cpl[3], NT)
+        for n, mask in enumerate(crowd):
+            remote(terms.at[n_crowd], terms.at[n], 6, 1, device(mask)).start()
+
+    def meet():
+        remote(early.at[pl.ds(0, n_crowd)], early.at[pl.ds(0, n_crowd)], 6, 0, me).wait_recv()
+        owns[...] = jnp.zeros_like(owns)
+        for n, mask in enumerate(crowd + [0]):
+            at = pl.ds(ordinal((2, 4, 5, 6), mask), 1)
+            owns[at] = owns[at] + early[n, 0:8, :][None]
+        lanes = lax.broadcasted_iota(jnp.int32, (TILE, TILE), 0).astype(F32)
+
+        def body(n, _):
+            row = early[n, 8:9, :]
+            lane = row - TILE * jnp.floor(row * (1.0 / TILE))
+            hots[n] = jnp.where(jnp.broadcast_to(lane, (TILE, TILE)) == lanes, 1.0, 0.0).astype(BF16)
+            return 0
+
+        lax.fori_loop(0, n_crowd + 1, body, 0, unroll=4)
+
+    def add_terms():
+        remote(terms.at[pl.ds(0, n_crowd)], terms.at[pl.ds(0, n_crowd)], 6, 1, me).wait_recv()
+        tiles = LEVELS[3].tiles
+        counts = lax.broadcasted_iota(jnp.int32, (tiles, 8, TILE), 0).astype(F32)
+
+        def one(n):
+            tile = jnp.floor(early[n, 8:9, :] * (1.0 / TILE))
+            hit = jnp.broadcast_to(tile[None], (tiles, 8, TILE)) == counts
+            return jnp.concatenate(
+                [
+                    jnp.where(hit, jnp.broadcast_to(v[None], (tiles, 8, TILE)), 0.0).reshape(tiles * 8, TILE)
+                    for v in halves(terms[n])
+                ],
+                axis=0,
+            ).astype(BF16)
+
+        def body(g, total):
+            left = jnp.concatenate([one(2 * g), one(2 * g + 1)], axis=1)
+            right = jnp.concatenate([hots[2 * g], hots[2 * g + 1]], axis=1)
+            return total + fast(left, right, NT)
+
+        both = lax.fori_loop(0, (n_crowd + 1) // 2, body, jnp.zeros((tiles * 16, TILE), F32), unroll=2)
+        half[...] = owns[...] + (both[: tiles * 8] + both[tiles * 8 :]).reshape(tiles, 8, TILE)
+        remote(half, other, 6, 2, device(1 << 4)).start()
+        remote(other, other, 6, 2, me).wait_recv()
+        top[...] = half[...] + other[...]
+
+        def finish():
+            remote(early.at[pl.ds(0, n_crowd)], early.at[pl.ds(0, n_crowd)], 6, 0, me).wait_send()
+            remote(terms.at[pl.ds(0, n_crowd)], terms.at[pl.ds(0, n_crowd)], 6, 1, me).wait_send()
+            remote(half, half, 6, 2, me).wait_send()
 
         leftover.append(finish)
 
@@ -284,23 +320,44 @@
     def coupled():
         cv[...] = dense(cpl[3], vmat[...], NT)
 
-    prepare(3)
-    scatter(3, base[3], bufs[6][0])
+    copies[0].wait()
+    copies[1].wait()
     pl.semaphore_wait(barrier, len(greet))
-
-    def others():
-        for k in (2, 1, 0):
-            prepare(k)
-
-    besides = {3: (others, inverse_blocks, coupled)}
-    first_copy = {3: 6, 2: 8, 1: 10, 0: 12}
+    introduce()
+
+    for n in range(2, 5):
+        copies[n].wait()
+    earlier = None
+    for j in range(4):
+        current = rhs[:, j * TILE : (j + 1) * TILE]
+        if j:
+            current = current - dense(earlier, sub[j - 1])
+        earlier = dense(current, inv[j])
+        fwd[:, j * TILE : (j + 1) * TILE] = earlier
+    copies[5].wait()
+    send_terms()
+    meet()
+    copies[6].wait()
+    prepare(2)
+    copies[7].wait()
+    copies[8].wait()
+    add_terms()
+
+    def beside_three():
+        prepare(1)
+        prepare(0)
+        prepare(3)
+        inverse_blocks()
+
+    besides = {2: beside_three, 1: coupled}
     for k in (3, 2, 1, 0):
-        total(k, 0, besides.get(k, (None, None, None)))
         m = LEVELS[k].own
-        copies[first_copy[k]].wait()
-        if k:
-            copies[first_copy[k] + 1].wait()
-        values = times_rows(k, bufs[2 * k][4])
+        if k < 3:
+            total(k, 0, besides.get(k))
+            copies[{2: 9, 1: 11, 0: 13}[k]].wait()
+            if k:
+                copies[{2: 10, 1: 12}[k]].wait()
+        values = times_rows(k, bufs[2 * k][4] if k < 3 else top)
         if k:
             term = base[k - 1]
             for q in range(m):
@@ -330,7 +387,7 @@
             if k == 3:
                 work[...] = dense(work[...], vmat[...], NT)
 
-        total(k, 1, (after, None, None))
+        total(k, 1, after)
         picked = gather(k, bufs[2 * k + 1][4])
     leaf_out[...] = work[...] - dense(picked, cv[...])
     sep_out[...] = sep_out[...] + dense(bufs[7][4][pl.ds(own_tile(3), 1)][0], select(3), NT)
@@ -343,17 +400,33 @@
     order = ins
     vmem = [pltpu.VMEM(x.shape, x.dtype) for x in order]
     bufs = []
-    for level in LEVELS:
+    for k, level in enumerate(LEVELS):
         w = level.share
+        n_crowd = 1 << len(SPARSE)
         shapes = (
             (level.tiles, 8, TILE),
-            (level.n_scatter - 1, w, 8, TILE),
+            ((1 << len(level.scatter)) - 1, w, 8, TILE),
             (w, 8, TILE),
-            (level.n_exchange - 1, w, 8, TILE),
+            ((1 << len(level.exchange)) - 1, w, 8, TILE),
             (level.tiles, 8, TILE),
         )
-        for _ in range(2):
-            bufs.append(tuple(pltpu.VMEM(s, F32) for s in shapes))
+        usual = tuple(pltpu.VMEM(s, F32) for s in shapes)
+        whole = pltpu.VMEM((level.tiles, 8, TILE), F32)
+        if k == 3:
+            bufs.append(
+                (
+                    pltpu.VMEM((n_crowd, 9, TILE), F32),
+                    pltpu.VMEM((n_crowd, 8, TILE), F32),
+                    pltpu.VMEM((n_crowd, TILE, TILE), BF16),
+                    whole,
+                    whole,
+                    whole,
+                    whole,
+                )
+            )
+        else:
+            bufs.append(usual)
+        bufs.append(usual)
     scratch = vmem + [
         pltpu.VMEM((8, 512), F32),
         pltpu.VMEM((4, 8, TILE), F32),
@@ -366,18 +439,18 @@
         pltpu.VMEM((8, 512), F32),
     ]
     sems = (
-        pltpu.SemaphoreType.DMA((13,)),
+        pltpu.SemaphoreType.DMA((14,)),
         pltpu.SemaphoreType.DMA((8, 3)),
         pltpu.SemaphoreType.DMA((8, 3)),
     )
     leaf, sep = pl.pallas_call(
         kernel,
         out_shape=(jax.ShapeDtypeStruct((8, 512), F32), jax.ShapeDtypeStruct((8, 96), F32)),
-        in_specs=[pl.BlockSpec(memory_space=pl.ANY)] * len(ins),
+        in_specs=[pl.BlockSpec(memory_space=pltpu.HBM)] * len(ins),
         out_specs=(pl.BlockSpec(memory_space=pltpu.VMEM),) * 2,
         scratch_shapes=scratch + bufs + [sems],
         compiler_params=pltpu.CompilerParams(
-            collective_id=0, has_side_effects=True, vmem_limit_bytes=40 * 1024 * 1024
+            collective_id=0, has_side_effects=True, vmem_limit_bytes=60 * 1024 * 1024
         ),
         name="nested_solve",
     )(*ins)

time: 168 us -> 146 us (0.87)
  Pallas kernels: 155 us -> 143 us
  local copies, waits for them, and re-layouts: 11.8 us -> 1.92 us
    pallas_call x1, Pallas kernels: 155 us -> 143 us  [local(): pl.pallas_call(kernel, out_shape=(jax.ShapeDtypeStruct((8, 512), F32), ja...]
    unnamed x28 -> x4, local copies, waits for them, and re-layouts: 11.8 us -> 1.92 us
where the time goes in v2:
time: 146 us; the launch traced here: 145 us
  Pallas kernels  143 us (98%)
  local copies, waits for them, and re-layouts  1.92 us (1%)
    pallas_call x1, Pallas kernels, local(): pl.pallas_call(kernel, out_shape=(jax.ShapeDtypeStruct((8, 512), F32), ja...  143 us

profile of v2, /device:TPU:1, one launch (start us, length us, event | category | flops | bytes accessed | tf_op | source)
XLA Modules:
  0.0 145.3 jit_solution(330372064528008598)
XLA Ops:
  0.6 142.8 %nested_solve.1 = (f32[8,512]{1,0:T(8,128)}, f32[8,96]{1,0:T(8,128)}) custom-call(f32[8,512]{1,0:T(8,128)} %bitcast.22, f32[4,128,128]{2,1,0:T(8,128)} %bitcast.18, f32[3,128,128]{2,1,0:T(8,128)} %bitcast.21, f32[8,96]{1,0:T(8,128)} %bitcast.27, s32[4,128]{1,0:T(4,128)} %bitcast.29, f32[4,128,512]{2,1,0:T(8,128)} %bitcast.15, f32[16,8192]{1,0:T(8,128)} %bitcast.16, ...), custom_call_target="tpu_custom_call" | custom-call | tf_op jit(solution)/shard_map/nested_solve/pallas_call | solution.py:446
  143.4 0.0 copy-start
  143.4 1.3 copy.17
  144.7 0.0 copy-done
  144.7 0.6 copy.18
Async XLA Ops:
  143.4 1.3 copy-start

commit v3 on v2

--- a/solution.py
+++ b/solution.py
@@ -49,6 +49,8 @@
 )
 SPARSE = (0, 1, 2, 5, 6)
 CORE = (4,)
+MID_SCATTER = (4,)
+MID_EXCHANGES = ((0, 1, 5), (2, 3))
 
 
 def hops(mask):
@@ -68,13 +70,14 @@
 def kernel(
     rhs_h, inv_h, sub_h, sep_h, pos_h, cpl_h, f1_h, f2_h, f3_h, f4_h, l2_h, l3_h, l4_h,
     leaf_out, sep_out,
-    rhs, inv, sub, sep, pos, cpl, f1, f2, f3, f4, l2, l3, l4,
-    fwd, base, place_t, place, owned, zval, vmat, cv, work,
+    rhs, inv, sub, sep, pos, cpl, f2, f3, f4, l2, l3, l4,
+    fwd, base, place_t, place, owned, zval, vmat, cv, work, cols,
     *rest,
 ):
     bufs = rest[:8]
-    in_sem, send_sem, recv_sem = rest[8][0], rest[8][1], rest[8][2]
-    factors = (f1, f2, f3, f4)
+    mids = rest[8]
+    in_sem, send_sem, recv_sem = rest[9]
+    factors = (None, f2, f3, f4)
     links = (l2, l3, l4)
 
     a, c = lax.axis_index("gx"), lax.axis_index("gy")
@@ -111,7 +114,7 @@
     pairs = (
         (sep_h, sep), (pos_h, pos), (rhs_h, rhs), (inv_h, inv), (sub_h, sub),
         (cpl_h.at[3], cpl.at[3]), (cpl_h.at[pl.ds(0, 3)], cpl.at[pl.ds(0, 3)]),
-        (f4_h, f4), (l4_h, l4), (f3_h, f3), (l3_h, l3), (f2_h, f2), (l2_h, l2), (f1_h, f1),
+        (f4_h, f4), (l4_h, l4), (f3_h, f3), (l3_h, l3), (f2_h, f2), (l2_h, l2),
     )
     copies = [pltpu.make_async_copy(s, d, in_sem.at[n]) for n, (s, d) in enumerate(pairs)]
     for copy in copies:
@@ -175,63 +178,126 @@
         got = fast(jnp.concatenate([high.astype(BF16), lo.astype(BF16)], axis=1), place_t[k])
         return jnp.sum(jnp.where(tile_of(k), got.reshape(tiles, 8, TILE), 0.0), axis=0)
 
-    def remote(src, dst, slot, phase, target):
+    def remote(src, dst, sem, target):
         return pltpu.make_async_remote_copy(
-            src_ref=src, dst_ref=dst, send_sem=send_sem.at[slot, phase], recv_sem=recv_sem.at[slot, phase],
+            src_ref=src, dst_ref=dst, send_sem=send_sem.at[sem], recv_sem=recv_sem.at[sem],
             device_id=target, device_id_type=MESH,
         )
 
     me = (a, c)
     leftover = []
 
-    def total(k, slot, beside=None):
+    def finish(ref, sem):
+        leftover.append(lambda: remote(ref, ref, sem, me).wait_send())
+
+    def arrive(ref, sem):
+        remote(ref, ref, sem, me).wait_recv()
+
+    def send_shares(part, got, bits, w, sem):
+        for n, mask in enumerate(masks_of(bits)):
+            theirs = pl.ds(ordinal(bits, mask) * w, w)
+            remote(part.at[theirs], got.at[n], sem, device(mask)).start()
+        finish(got, sem)
+
+    def send_all(ref, seen, bits, sem):
+        for n, mask in enumerate(masks_of(bits)):
+            remote(ref, seen.at[n], sem, device(mask)).start()
+        finish(seen, sem)
+
+    def send_mine(full, bits, w, sem):
+        at = pl.ds(ordinal(bits) * w, w)
+        for mask in masks_of(bits):
+            remote(full.at[at], full.at[at], sem, device(mask)).start()
+        finish(full.at[pl.ds(0, full.shape[0] - w)], sem)
+
+    def combine(k, slot, beside=None, spare=None):
         level = LEVELS[k]
         w = level.share
-        part, got, mine, seen, full = bufs[2 * k + slot]
-        s = 2 * k + slot
-        at = pl.ds(ordinal(level.scatter) * w, w)
-        peers = masks_of(level.scatter)
-        for n, mask in enumerate(peers):
-            theirs = pl.ds(ordinal(level.scatter, mask) * w, w)
-            remote(part.at[theirs], got.at[n], s, 0, device(mask)).start()
+        part, got, mine, seen = bufs[2 * k + slot][:4]
+        s = 3 * (2 * k + slot)
+        if not slot:
+            send_shares(part, got, level.scatter, w, s)
         if beside:
             beside()
-        remote(got, got, s, 0, me).wait_recv()
-        mine[...] = part[at] + jnp.sum(got[...], axis=0)
-        for n, mask in enumerate(masks_of(level.exchange)):
-            remote(mine, seen.at[n], s, 1, device(mask)).start()
-        remote(seen, seen, s, 1, me).wait_recv()
-        full[at] = mine[...] + jnp.sum(seen[...], axis=0)
-        for mask in peers:
-            remote(full.at[at], full.at[at], s, 2, device(mask)).start()
-        others = full.at[pl.ds(0, level.tiles - w)]
-        remote(others, others, s, 2, me).wait_recv()
-
-        def finish():
-            remote(others, others, s, 0, me).wait_send()
-            remote(seen, seen, s, 1, me).wait_send()
-            remote(got, got, s, 2, me).wait_send()
-
-        leftover.append(finish)
+        arrive(got, s)
+        mine[...] = part[pl.ds(ordinal(level.scatter) * w, w)] + jnp.sum(got[...], axis=0)
+        return swap(k, slot, spare)
+
+    def swap(k, slot, spare=None):
+        mine, seen = bufs[2 * k + slot][2:4]
+        s = 3 * (2 * k + slot) + 1
+        send_all(mine, seen, LEVELS[k].exchange, s)
+        if spare:
+            spare()
+        arrive(seen, s)
+        return mine[...] + jnp.sum(seen[...], axis=0)
+
+    def spread_out(k, slot, value):
+        level = LEVELS[k]
+        w = level.share
+        full = bufs[2 * k + slot][4]
+        s = 3 * (2 * k + slot) + 2
+        full[pl.ds(ordinal(level.scatter) * w, w)] = value
+        send_mine(full, level.scatter, w, s)
+        arrive(full.at[pl.ds(0, level.tiles - w)], s)
+
+    top_bits = LEVELS[0].scatter
+    n_top = 1 << len(top_bits)
+
+    def columns(mask=0):
+        return pl.ds(pl.multiple_of(ordinal(top_bits, mask) * TILE, TILE), TILE)
+
+    def send_columns():
+        mine = cols.at[ordinal(top_bits)]
+        pltpu.make_async_copy(f1_h.at[:, columns()], mine, in_sem.at[13]).start()
+        for mask in masks_of(top_bits):
+            remote(f1_h.at[:, columns(mask)], mine, 24, device(mask)).start()
+        finish(cols.at[pl.ds(0, n_top - 1)], 24)
+
+    def columns_here():
+        pltpu.make_async_copy(f1_h.at[:, columns()], cols.at[ordinal(top_bits)], in_sem.at[13]).wait()
+        arrive(cols.at[pl.ds(0, n_top - 1)], 24)
+
+    def middle(tile):
+        rows = n_top * LEVELS[0].own
+        part = dense(tile, cols[...].reshape(rows, TILE), NT)
+        zbuf, zgot, zmine, zseen, znext, zlast, zfull = mids
+        n = rows // TILE
+        for j in range(n):
+            zbuf[j] = part[:, j * TILE : (j + 1) * TILE]
+        w = n >> len(MID_SCATTER)
+        at = pl.ds(ordinal(MID_SCATTER) * w, w)
+        send_shares(zbuf, zgot, MID_SCATTER, w, 25)
+        arrive(zgot, 25)
+        zmine[...] = zbuf[at] + jnp.sum(zgot[...], axis=0)
+        send_all(zmine, zseen, MID_EXCHANGES[0], 26)
+        arrive(zseen, 26)
+        znext[...] = zmine[...] + jnp.sum(zseen[...], axis=0)
+        send_all(znext, zlast, MID_EXCHANGES[1], 28)
+        arrive(zlast, 28)
+        zfull[at] = znext[...] + jnp.sum(zlast[...], axis=0)
+        send_mine(zfull, MID_SCATTER, w, 27)
+        arrive(zfull.at[pl.ds(0, n - w)], 27)
+        whole = jnp.concatenate([zfull[j] for j in range(n)], axis=1)
+        return dense(whole, cols[...].reshape(rows, TILE))
 
     crowd = masks_of(SPARSE)
     n_crowd = len(crowd)
     early, terms, hots, owns, half, other, top = bufs[6]
 
     def introduce():
-        owned_row = dense(sep[...], select(3))
-        early[n_crowd, 0:8, :] = owned_row
-        early[n_crowd, 8:9, :] = pos[3:4, :].astype(F32)
         for n, mask in enumerate(crowd):
-            remote(early.at[n_crowd], early.at[n], 6, 0, device(mask)).start()
+            remote(early.at[n_crowd], early.at[n], 18, device(mask)).start()
+        finish(early.at[pl.ds(0, n_crowd)], 18)
 
     def send_terms():
         terms[n_crowd] = -dense(fwd[...], cpl[3], NT)
         for n, mask in enumerate(crowd):
-            remote(terms.at[n_crowd], terms.at[n], 6, 1, device(mask)).start()
+            remote(terms.at[n_crowd], terms.at[n], 19, device(mask)).start()
+        finish(terms.at[pl.ds(0, n_crowd)], 19)
 
     def meet():
-        remote(early.at[pl.ds(0, n_crowd)], early.at[pl.ds(0, n_crowd)], 6, 0, me).wait_recv()
+        arrive(early.at[pl.ds(0, n_crowd)], 18)
         owns[...] = jnp.zeros_like(owns)
         for n, mask in enumerate(crowd + [0]):
             at = pl.ds(ordinal((2, 4, 5, 6), mask), 1)
@@ -247,7 +313,7 @@
         lax.fori_loop(0, n_crowd + 1, body, 0, unroll=4)
 
     def add_terms():
-        remote(terms.at[pl.ds(0, n_crowd)], terms.at[pl.ds(0, n_crowd)], 6, 1, me).wait_recv()
+        arrive(terms.at[pl.ds(0, n_crowd)], 19)
         tiles = LEVELS[3].tiles
         counts = lax.broadcasted_iota(jnp.int32, (tiles, 8, TILE), 0).astype(F32)
 
@@ -269,16 +335,10 @@
 
         both = lax.fori_loop(0, (n_crowd + 1) // 2, body, jnp.zeros((tiles * 16, TILE), F32), unroll=2)
         half[...] = owns[...] + (both[: tiles * 8] + both[tiles * 8 :]).reshape(tiles, 8, TILE)
-        remote(half, other, 6, 2, device(1 << 4)).start()
-        remote(other, other, 6, 2, me).wait_recv()
+        remote(half, other, 20, device(1 << 4)).start()
+        finish(half, 20)
+        arrive(other, 20)
         top[...] = half[...] + other[...]
-
-        def finish():
-            remote(early.at[pl.ds(0, n_crowd)], early.at[pl.ds(0, n_crowd)], 6, 0, me).wait_send()
-            remote(terms.at[pl.ds(0, n_crowd)], terms.at[pl.ds(0, n_crowd)], 6, 1, me).wait_send()
-            remote(half, half, 6, 2, me).wait_send()
-
-        leftover.append(finish)
 
     def times_rows(k, full):
         factor = factors[k]
@@ -291,6 +351,30 @@
 
         sums = lax.fori_loop(0, LEVELS[k].tiles, body, tuple(jnp.zeros((8, TILE), F32) for _ in range(m)), unroll=4)
         return [jnp.sum(v, axis=1, keepdims=True) for v in sums]
+
+    def spread_share(k, wide, out, place):
+        factor = factors[k]
+        w = LEVELS[k].share
+        for j in range(w):
+            tile = place * w + j
+            rows = factor[:, pl.ds(pl.multiple_of(tile * TILE, TILE), TILE)]
+            acc = wide[0] * rows[0:1, :]
+            for q in range(1, LEVELS[k].own):
+                acc = acc + wide[q] * rows[q : q + 1, :]
+            out[tile] = acc
+
+    def spread_send(k, values):
+        part, got = bufs[2 * k + 1][:2]
+        bits = LEVELS[k].scatter
+        w = LEVELS[k].share
+        s = 3 * (2 * k + 1)
+        wide = [jnp.broadcast_to(v, (8, TILE)) for v in values]
+        for n, mask in enumerate(masks_of(bits)):
+            place = ordinal(bits, mask)
+            spread_share(k, wide, part, place)
+            remote(part.at[pl.ds(place * w, w)], got.at[n], s, device(mask)).start()
+        spread_share(k, wide, part, ordinal(bits))
+        finish(got, s)
 
     def spread(k, values, out):
         factor = factors[k]
@@ -320,13 +404,13 @@
     def coupled():
         cv[...] = dense(cpl[3], vmat[...], NT)
 
-    copies[0].wait()
-    copies[1].wait()
+    for n in range(6):
+        copies[n].wait()
+    early[n_crowd, 0:8, :] = dense(sep[...], select(3))
+    early[n_crowd, 8:9, :] = pos[3:4, :].astype(F32)
     pl.semaphore_wait(barrier, len(greet))
     introduce()
 
-    for n in range(2, 5):
-        copies[n].wait()
     earlier = None
     for j in range(4):
         current = rhs[:, j * TILE : (j + 1) * TILE]
@@ -334,7 +418,6 @@
             current = current - dense(earlier, sub[j - 1])
         earlier = dense(current, inv[j])
         fwd[:, j * TILE : (j + 1) * TILE] = earlier
-    copies[5].wait()
     send_terms()
     meet()
     copies[6].wait()
@@ -349,22 +432,29 @@
         prepare(3)
         inverse_blocks()
 
-    besides = {2: beside_three, 1: coupled}
+    values = None
     for k in (3, 2, 1, 0):
         m = LEVELS[k].own
+        full = top
+        if k == 2:
+            value = combine(2, 0, beside_three)
+        elif k == 1:
+            value = combine(1, 0, coupled, send_columns)
+        elif k == 0:
+            bufs[1][2][...] = middle(combine(0, 0, columns_here)[0])[None]
+            break
         if k < 3:
-            total(k, 0, besides.get(k))
-            copies[{2: 9, 1: 11, 0: 13}[k]].wait()
-            if k:
-                copies[{2: 10, 1: 12}[k]].wait()
-        values = times_rows(k, bufs[2 * k][4] if k < 3 else top)
-        if k:
-            term = base[k - 1]
-            for q in range(m):
-                term = term + values[q] * links[k - 1][q : q + 1, :]
-            scatter(k - 1, term, bufs[2 * (k - 1)][0])
-            for q in range(m):
-                zval[LEVELS[k].off + q] = jnp.broadcast_to(values[q], (8, TILE))
+            spread_out(k, 0, value)
+            full = bufs[2 * k][4]
+            copies[{2: 9, 1: 11}[k]].wait()
+            copies[{2: 10, 1: 12}[k]].wait()
+        values = times_rows(k, full)
+        term = base[k - 1]
+        for q in range(m):
+            term = term + values[q] * links[k - 1][q : q + 1, :]
+        scatter(k - 1, term, bufs[2 * (k - 1)][0])
+        for q in range(m):
+            zval[LEVELS[k].off + q] = jnp.broadcast_to(values[q], (8, TILE))
 
     picked = None
     for k in range(4):
@@ -375,7 +465,7 @@
                 - jnp.sum(picked * links[k - 1][q : q + 1, :], axis=1, keepdims=True)
                 for q in range(m)
             ]
-        spread(k, values, bufs[2 * k + 1][0])
+            spread_send(k, values)
 
         def after(k=k, picked=picked):
             if k == 0:
@@ -387,18 +477,18 @@
             if k == 3:
                 work[...] = dense(work[...], vmat[...], NT)
 
-        total(k, 1, after)
+        value = combine(k, 1, after) if k else swap(0, 1, after)
+        spread_out(k, 1, value)
         picked = gather(k, bufs[2 * k + 1][4])
     leaf_out[...] = work[...] - dense(picked, cv[...])
     sep_out[...] = sep_out[...] + dense(bufs[7][4][pl.ds(own_tile(3), 1)][0], select(3), NT)
-    for finish in leftover:
-        finish()
+    for sent in leftover:
+        sent()
 
 
 def local(*args):
     ins = [x[0, 0] for x in args]
-    order = ins
-    vmem = [pltpu.VMEM(x.shape, x.dtype) for x in order]
+    vmem = [pltpu.VMEM(x.shape, x.dtype) for n, x in enumerate(ins) if n != 6]
     bufs = []
     for k, level in enumerate(LEVELS):
         w = level.share
@@ -437,18 +527,33 @@
         pltpu.VMEM((512, 512), F32),
         pltpu.VMEM((TILE, 512), F32),
         pltpu.VMEM((8, 512), F32),
+        pltpu.VMEM((1 << len(LEVELS[0].scatter), LEVELS[0].own, TILE), F32),
     ]
+    n = (LEVELS[0].own << len(LEVELS[0].scatter)) // TILE
+    w = n >> len(MID_SCATTER)
+    mids = tuple(
+        pltpu.VMEM(s + (8, TILE), F32)
+        for s in (
+            (n,),
+            ((1 << len(MID_SCATTER)) - 1, w),
+            (w,),
+            ((1 << len(MID_EXCHANGES[0])) - 1, w),
+            (w,),
+            ((1 << len(MID_EXCHANGES[1])) - 1, w),
+            (n,),
+        )
+    )
     sems = (
         pltpu.SemaphoreType.DMA((14,)),
-        pltpu.SemaphoreType.DMA((8, 3)),
-        pltpu.SemaphoreType.DMA((8, 3)),
+        pltpu.SemaphoreType.DMA((32,)),
+        pltpu.SemaphoreType.DMA((32,)),
     )
     leaf, sep = pl.pallas_call(
         kernel,
         out_shape=(jax.ShapeDtypeStruct((8, 512), F32), jax.ShapeDtypeStruct((8, 96), F32)),
         in_specs=[pl.BlockSpec(memory_space=pltpu.HBM)] * len(ins),
         out_specs=(pl.BlockSpec(memory_space=pltpu.VMEM),) * 2,
-        scratch_shapes=scratch + bufs + [sems],
+        scratch_shapes=scratch + bufs + [mids, sems],
         compiler_params=pltpu.CompilerParams(
             collective_id=0, has_side_effects=True, vmem_limit_bytes=60 * 1024 * 1024
         ),

time: 146 us -> 143 us (0.979)
  Pallas kernels: 143 us -> 140 us
    pallas_call x1, Pallas kernels: 143 us -> 140 us  [local(): pl.pallas_call(kernel, out_shape=(jax.ShapeDtypeStruct((8, 512), F32), ja...]
where the time goes in v3:
time: 143 us
  Pallas kernels  140 us (98%)
  local copies, waits for them, and re-layouts  1.92 us (1%)
    pallas_call x1, Pallas kernels, local(): pl.pallas_call(kernel, out_shape=(jax.ShapeDtypeStruct((8, 512), F32), ja...  140 us

profile of v3, /device:TPU:1, one launch (start us, length us, event | category | flops | bytes accessed | tf_op | source)
XLA Modules:
  0.0 142.6 jit_solution(157801621010760912)
XLA Ops:
  0.6 140.0 %nested_solve.1 = (f32[8,512]{1,0:T(8,128)}, f32[8,96]{1,0:T(8,128)}) custom-call(f32[8,512]{1,0:T(8,128)} %bitcast.22, f32[4,128,128]{2,1,0:T(8,128)} %bitcast.18, f32[3,128,128]{2,1,0:T(8,128)} %bitcast.21, f32[8,96]{1,0:T(8,128)} %bitcast.27, s32[4,128]{1,0:T(4,128)} %bitcast.29, f32[4,128,512]{2,1,0:T(8,128)} %bitcast.15, f32[16,8192]{1,0:T(8,128)} %bitcast.16, ...), custom_call_target="tpu_custom_call" | custom-call | tf_op jit(solution)/shard_map/nested_solve/pallas_call | solution.py:551
  140.6 0.0 copy-start
  140.6 1.3 copy.17
  142.0 0.0 copy-done
  142.0 0.6 copy.18
Async XLA Ops:
  140.6 1.3 copy-start

commit v4 on v3

--- a/solution.py
+++ b/solution.py
@@ -291,7 +291,6 @@
         finish(early.at[pl.ds(0, n_crowd)], 18)
 
     def send_terms():
-        terms[n_crowd] = -dense(fwd[...], cpl[3], NT)
         for n, mask in enumerate(crowd):
             remote(terms.at[n_crowd], terms.at[n], 19, device(mask)).start()
         finish(terms.at[pl.ds(0, n_crowd)], 19)
@@ -333,7 +332,7 @@
             right = jnp.concatenate([hots[2 * g], hots[2 * g + 1]], axis=1)
             return total + fast(left, right, NT)
 
-        both = lax.fori_loop(0, (n_crowd + 1) // 2, body, jnp.zeros((tiles * 16, TILE), F32), unroll=2)
+        both = lax.fori_loop(0, (n_crowd + 1) // 2, body, jnp.zeros((tiles * 16, TILE), F32), unroll=8)
         half[...] = owns[...] + (both[: tiles * 8] + both[tiles * 8 :]).reshape(tiles, 8, TILE)
         remote(half, other, 20, device(1 << 4)).start()
         finish(half, 20)
@@ -349,7 +348,7 @@
             rows = factor[:, pl.ds(pl.multiple_of(j * TILE, TILE), TILE)]
             return tuple(sums[q] + tile * rows[q : q + 1, :] for q in range(m))
 
-        sums = lax.fori_loop(0, LEVELS[k].tiles, body, tuple(jnp.zeros((8, TILE), F32) for _ in range(m)), unroll=4)
+        sums = lax.fori_loop(0, LEVELS[k].tiles, body, tuple(jnp.zeros((8, TILE), F32) for _ in range(m)), unroll=16)
         return [jnp.sum(v, axis=1, keepdims=True) for v in sums]
 
     def spread_share(k, wide, out, place):
@@ -408,9 +407,6 @@
         copies[n].wait()
     early[n_crowd, 0:8, :] = dense(sep[...], select(3))
     early[n_crowd, 8:9, :] = pos[3:4, :].astype(F32)
-    pl.semaphore_wait(barrier, len(greet))
-    introduce()
-
     earlier = None
     for j in range(4):
         current = rhs[:, j * TILE : (j + 1) * TILE]
@@ -418,6 +414,9 @@
             current = current - dense(earlier, sub[j - 1])
         earlier = dense(current, inv[j])
         fwd[:, j * TILE : (j + 1) * TILE] = earlier
+    terms[n_crowd] = -dense(fwd[...], cpl[3], NT)
+    pl.semaphore_wait(barrier, len(greet))
+    introduce()
     send_terms()
     meet()
     copies[6].wait()
@@ -437,11 +436,11 @@
         m = LEVELS[k].own
         full = top
         if k == 2:
-            value = combine(2, 0, beside_three)
+            value = combine(2, 0, beside_three, send_columns)
         elif k == 1:
-            value = combine(1, 0, coupled, send_columns)
+            value = combine(1, 0)
         elif k == 0:
-            bufs[1][2][...] = middle(combine(0, 0, columns_here)[0])[None]
+            bufs[1][2][...] = middle(combine(0, 0, coupled, columns_here)[0])[None]
             break
         if k < 3:
             spread_out(k, 0, value)

time: 143 us -> 141 us (0.986)
  no operation moved by 1% of the time
where the time goes in v4:
time: 141 us
  Pallas kernels  139 us (99%)
  local copies, waits for them, and re-layouts  1.92 us (1%)
    pallas_call x1, Pallas kernels, local(): pl.pallas_call(kernel, out_shape=(jax.ShapeDtypeStruct((8, 512), F32), ja...  139 us

profile of v4, /device:TPU:1, one launch (start us, length us, event | category | flops | bytes accessed | tf_op | source)
XLA Modules:
  0.0 141.3 jit_solution(14593162344602397752)
XLA Ops:
  0.6 138.7 %nested_solve.1 = (f32[8,512]{1,0:T(8,128)}, f32[8,96]{1,0:T(8,128)}) custom-call(f32[8,512]{1,0:T(8,128)} %bitcast.22, f32[4,128,128]{2,1,0:T(8,128)} %bitcast.18, f32[3,128,128]{2,1,0:T(8,128)} %bitcast.21, f32[8,96]{1,0:T(8,128)} %bitcast.27, s32[4,128]{1,0:T(4,128)} %bitcast.29, f32[4,128,512]{2,1,0:T(8,128)} %bitcast.15, f32[16,8192]{1,0:T(8,128)} %bitcast.16, ...), custom_call_target="tpu_custom_call" | custom-call | tf_op jit(solution)/shard_map/nested_solve/pallas_call | solution.py:550
  139.4 0.0 copy-start
  139.4 1.3 copy.17
  140.7 0.0 copy-done
  140.7 0.6 copy.18
Async XLA Ops:
  139.4 1.3 copy-start
